TPU v7x, 128 devices: a whole 4x4x4 slice. The times are simulated.
128 devices in a mesh: fsdp: 32 (over z, x, core), feat: 4 (over y).
Axes of the slice: x: 4, y: 4, z: 4, core: 2. Of those that a mesh axis runs over, the one named last changes fastest.
Arguments:
- table_cells: bfloat16 [1536, 256, 192], P(('fsdp', 'feat'))
- attn_weights: bfloat16 [8, 192, 192], P(None, 'fsdp')
- hidden_up_weight: bfloat16 [192, 384], P('fsdp'), may hold values from -0.4375 to 0.4375
- hidden_down_weight: bfloat16 [384, 192], P('fsdp'), may hold values from -0.3125 to 0.3125
- norm_gains: float32 [3, 192], replicated, may hold values from 0.25 to 1.75
- train_count: int32 [1], replicated, may hold values from 384 to 1152
- feature_count: int32 [1], replicated, may hold values from 128 to 256
Outputs:
- layer_out: bfloat16 [1536, 256, 192], P(('fsdp', 'feat'))
Inputs may be any that keep to these rules, and one draw needn't show every extreme that they name: Rows 0 to train_count - 1 are the training rows. Features 0 to feature_count - 1 are real, the others padding.
All inputs are finite; a program needn't handle non-finite values.
Results may differ from a plain program's by a relative error of at most 0.012.
The roundings to bfloat16 on the way count: a program that leaves them out, or rounds other values in their place, can miss the bound.
Values may be sent and summed in bfloat16 or wider, within the bound.
A program may use at most 128 MiB of HBM per device.

v0:
```python
import jax
import jax.numpy as jnp
from jax import lax
from jax.sharding import PartitionSpec as P

HEADS = 6
EPS = 1e-05
NEGATIVE = -1e30


def normalize(value_rows, gain):
    floats = value_rows.astype(jnp.float32)
    average = jnp.mean(floats, axis=-1, keepdims=True)
    centered = floats - average
    variance = jnp.mean(centered * centered, axis=-1, keepdims=True)
    return (centered * lax.rsqrt(variance + EPS) * gain).astype(jnp.bfloat16)


def softmax_rows(scores, live):
    masked = jnp.where(live, scores, NEGATIVE)
    row_maximum = jnp.max(masked, axis=-1, keepdims=True)
    exponent = jnp.exp(masked - row_maximum)
    return (exponent / jnp.sum(exponent, axis=-1, keepdims=True)).astype(jnp.bfloat16)


def project(normed, weight):
    model_width = normed.shape[-1]
    product = jnp.dot(normed.reshape(-1, model_width), weight, preferred_element_type=jnp.float32)
    return product.astype(jnp.bfloat16).reshape(normed.shape[:-1] + (weight.shape[1],))


def output_proj(attended_rows, residual, weight):
    model_width = attended_rows.shape[-1]
    product = jnp.dot(
        attended_rows.reshape(-1, model_width), weight, preferred_element_type=jnp.float32
    )
    return (residual.astype(jnp.float32) + product.reshape(residual.shape)).astype(jnp.bfloat16)


def feature_attention(table_cells, normed, weights, feat_live):
    model_width = normed.shape[-1]
    head_size = model_width // HEADS
    queries = project(normed, weights[0])
    keys = project(normed, weights[1])
    value_rows = project(normed, weights[2])
    outputs = []
    for index_head in range(HEADS):
        training_extent = slice(index_head * head_size, (index_head + 1) * head_size)
        scores = jnp.einsum(
            "rqe,rke->rqk",
            queries[..., training_extent],
            keys[..., training_extent],
            preferred_element_type=jnp.float32,
        ) * head_size ** (-0.5)
        attention_probabilities = softmax_rows(scores, feat_live[None, None, :])
        outputs.append(
            jnp.einsum(
                "rqk,rke->rqe",
                attention_probabilities,
                value_rows[..., training_extent],
                preferred_element_type=jnp.float32,
            ).astype(jnp.bfloat16)
        )
    return output_proj(jnp.concatenate(outputs, axis=-1), table_cells, weights[3])


def sample_attention(column_block, normed, weights, row_live):
    all_rows, feat_here, model_width = normed.shape
    head_size = model_width // HEADS
    queries = project(normed, weights[4])
    keys = project(normed, weights[5])
    value_rows = project(normed, weights[6])
    block_count = max(1, all_rows // 512)
    block_rows = all_rows // block_count
    query_blocks = queries.reshape(block_count, block_rows, feat_here, model_width)

    def one_block(query_block):
        outputs = []
        for index_head in range(HEADS):
            training_extent = slice(index_head * head_size, (index_head + 1) * head_size)
            scores = jnp.einsum(
                "vsg,psg->svp",
                query_block[..., training_extent],
                keys[..., training_extent],
                preferred_element_type=jnp.float32,
            ) * head_size ** (-0.5)
            attention_probabilities = softmax_rows(scores, row_live[None, None, :])
            outputs.append(
                jnp.einsum(
                    "tdj,jtn->dtn",
                    attention_probabilities,
                    value_rows[..., training_extent],
                    preferred_element_type=jnp.float32,
                ).astype(jnp.bfloat16)
            )
        return jnp.concatenate(outputs, axis=-1)

    attended_rows = lax.map(one_block, query_blocks).reshape(all_rows, feat_here, model_width)
    return output_proj(attended_rows, column_block, weights[7])


def feed_forward(value_rows, gain, w_in, w_out):
    model_width = value_rows.shape[-1]
    normed = normalize(value_rows, gain)
    hidden = jnp.dot(normed.reshape(-1, model_width), w_in, preferred_element_type=jnp.float32)
    activated = jax.nn.gelu(hidden).astype(jnp.bfloat16)
    result = value_rows.astype(jnp.float32) + jnp.dot(
        activated, w_out, preferred_element_type=jnp.float32
    ).reshape(value_rows.shape)
    return result.astype(jnp.bfloat16)


def local(
    table_cells,
    attn_weights,
    hidden_up_weight,
    hidden_down_weight,
    norm_gains,
    train_count,
    feature_count,
):
    weights, w_in, w_out = (
        lax.all_gather(attn_weights, "fsdp", axis=1, tiled=True),
        lax.all_gather(hidden_up_weight, "fsdp", axis=0, tiled=True),
        lax.all_gather(hidden_down_weight, "fsdp", axis=0, tiled=True),
    )
    feat_live = jnp.arange(table_cells.shape[1]) < feature_count[0]
    normed_one = normalize(table_cells, norm_gains[0])
    mixed_rows = feature_attention(table_cells, normed_one, weights, feat_live)
    fsdp_size = lax.axis_size("fsdp")
    groups = lax.axis_size("feat")
    row_dev, feat_total, model_width = table_cells.shape
    devices_all = fsdp_size * groups
    all_rows = row_dev * devices_all
    train_limit = train_count[0]
    row_index = jnp.arange(all_rows)
    split_cells = mixed_rows.reshape(row_dev, devices_all, feat_total // devices_all, model_width)
    column_block = lax.all_to_all(
        split_cells, ("fsdp", "feat"), split_axis=1, concat_axis=0, tiled=True
    )
    rows_here, single, feat_here, width_here = column_block.shape
    owner_column_block = column_block.reshape(rows_here, feat_here, width_here)
    normed_two = normalize(owner_column_block, norm_gains[1])
    sampled = sample_attention(owner_column_block, normed_two, weights, row_index < train_limit)
    at_owners = sampled.reshape(rows_here, single, feat_here, width_here)
    returned = lax.all_to_all(at_owners, ("fsdp", "feat"), split_axis=0, concat_axis=1, tiled=True)
    returned = returned.reshape(row_dev, feat_total, model_width)
    returned = feed_forward(returned, norm_gains[2], w_in, w_out)
    return returned


def solution(mesh):
    in_specs = (
        P(("fsdp", "feat"), None, None),
        P(None, "fsdp", None),
        P("fsdp", None),
        P("fsdp", None),
        P(),
        P(),
        P(),
    )
    out_specs = P(("fsdp", "feat"), None, None)
    return jax.shard_map(local, mesh=mesh, in_specs=in_specs, out_specs=out_specs, check_vma=False)
```

profile of v0, /device:TPU:1, one launch (start us, length us, event | category | flops | bytes accessed | tf_op | source)
XLA Modules:
  0.0 370.8 jit_solution(5374347418670035218)
XLA Ops:
  0.0 27.7 %all_gather.9 = bf16[8,192,192]{2,0,1:T(8,128)(2,1)S(1)} all-gather(bf16[8,6,192]{2,0,1:T(8,128)(2,1)} %param.10), channel_id=1, replica_groups=mesh['fsdp'=32,'feat'=4] {'fsdp'}, dimensions={1}, use_global_device_ids=true | all-gather | bytes 608256 | tf_op jit(solution)/shard_map/all_gather | solution.py:123
  47.1 3.9 %fusion.417 = (f32[12,256]{1,0:T(8,128)S(1)}, f32[12,256,256]{1,2,0:T(8,128)}) fusion(pred[256]{0:T(512)(128)(4,1)S(1)} %iota_compare_fusion.1, bf16[12,256,32]{1,0,2:T(8,128)(2,1)} %get-tuple-element.136, bf16[12,256,32]{1,0,2:T(8,128)(2,1)} %get-tuple-element.106), kind=kOutput, calls=%fused_computation.353 | convolution fusion | flops 53477632 | bytes 3551488 | tf_op jit(solution)/shard_map/sub | solution.py:22
  51.0 4.0 %fusion.426 = (f32[12,256]{1,0:T(8,128)S(1)}, f32[12,256,256]{1,2,0:T(8,128)}) fusion(pred[256]{0:T(512)(128)(4,1)S(1)} %iota_compare_fusion.1, bf16[12,256,32]{1,0,2:T(8,128)(2,1)} %get-tuple-element.137, bf16[12,256,32]{1,0,2:T(8,128)(2,1)} %get-tuple-element.105), kind=kOutput, calls=%fused_computation.354 | convolution fusion | flops 53477632 | bytes 3551488 | tf_op jit(solution)/shard_map/sub | solution.py:22
  55.0 4.0 %fusion.435 = (f32[12,256]{1,0:T(8,128)S(1)}, f32[12,256,256]{1,2,0:T(8,128)}) fusion(pred[256]{0:T(512)(128)(4,1)S(1)} %iota_compare_fusion.1, bf16[12,256,32]{1,0,2:T(8,128)(2,1)} %get-tuple-element.138, bf16[12,256,32]{1,0,2:T(8,128)(2,1)} %get-tuple-element.104), kind=kOutput, calls=%fused_computation.355 | convolution fusion | flops 53477632 | bytes 3551488 | tf_op jit(solution)/shard_map/sub | solution.py:22
  84.9 7.2 %all-to-all-start = ((bf16[12,128,2,192]{3,2,0,1:T(2,128)(2,1)}), bf16[12,128,2,192]{3,2,0,1:T(2,128)(2,1)S(1)}, u32[]{:S(2)}, u32[]{:S(2)}) async-start(bf16[12,128,2,192]{3,2,0,1:T(2,128)(2,1)} %copy.182), calls=%async_computation | async-start | bytes 3145728 | tf_op jit(solution)/shard_map/all_to_all | solution.py:138
  92.9 24.1 %all-to-all-done = bf16[12,128,2,192]{3,2,0,1:T(2,128)(2,1)S(1)} async-done(((bf16[12,128,2,192]{3,2,0,1:T(2,128)(2,1)}), bf16[12,128,2,192]{3,2,0,1:T(2,128)(2,1)S(1)}, u32[]{:S(2)}, u32[]{:S(2)}) %all-to-all-start) | async-done | bytes 1179680 | tf_op jit(solution)/shard_map/all_to_all | solution.py:138
  118.9 4.0 %multiply_reduce_fusion.1 = f32[128,12,2]{2,1,0:T(8,128)S(1)} fusion(bf16[12,128,2,192]{3,2,0,1:T(2,128)(2,1)S(1)} %all-to-all-done, f32[128,12,2]{2,1,0:T(8,128)S(1)} %broadcast_multiply_fusion.1), kind=kLoop, calls=%fused_computation.190 | loop fusion | flops 2356224 | bytes 1204224 | tf_op jit(solution)/shard_map/reduce_sum | solution.py:15
  123.1 3.9 %multiply_convert_fusion.1 = bf16[128,12,1,2,192]{4,3,1,0,2:T(2,128)(2,1)S(1)} fusion(bf16[12,128,2,192]{3,2,0,1:T(2,128)(2,1)S(1)} %all-to-all-done, f32[192]{0:T(256)S(1)} %bitcast.148, f32[128,12,2]{2,1,0:T(8,128)S(1)} %add_rsqrt_fusion.1, f32[128,12,2]{2,1,0:T(8,128)S(1)} %broadcast_multiply_fusion.1), kind=kLoop, calls=%fused_computation.189 | loop fusion | flops 2949120 | bytes 2384640 | tf_op jit(solution)/shard_map/convert_element_type | solution.py:16
  134.0 4.9 %copy.190 = bf16[1536,2,192]{0,2,1:T(8,128)(2,1)} copy(bf16[1536,2,192]{2,1,0:T(2,128)(2,1)} %reshape.234) | data formatting | bytes 2359296
  144.4 4.9 %copy.191 = bf16[1536,2,192]{0,2,1:T(8,128)(2,1)} copy(bf16[1536,2,192]{2,1,0:T(2,128)(2,1)} %reshape.235) | data formatting | bytes 2359296
  152.6 105.7 %while.11 = (s32[]{:T(128)}, bf16[3,512,2,192]{1,3,2,0:T(8,128)(2,1)}, bf16[3,512,2,192]{1,3,2,0:T(8,128)(2,1)S(1)}, bf16[1536,2,192]{0,2,1:T(8,128)(2,1)}, bf16...) while((s32[]{:T(128)}, bf16[3,512,2,192]{1,3,2,0:T(8,128)(2,1)}, ...), condition=%wide.region_29.30_spmd.clone, body=%wide.region_16.29_spmd.clone.sunk | while | flops 1897096704 | bytes 11085937 | solution.py:98
  162.1 3.3 fusion.556
  167.5 3.3 fusion.558
  172.9 3.3 fusion.560
  197.1 3.3 fusion.556
  232.2 3.3 fusion.556
  262.0 3.3 copy.194
  270.7 3.9 %all-to-all-start.1 = ((bf16[1536,1,2,192]{3,2,1,0:T(2,128)(2,1)}), bf16[1536,1,2,192]{3,2,1,0:T(2,128)(2,1)S(1)}, u32[]{:S(2)}, u32[]{:S(2)}) async-start(bf16[1536,1,2,192]{3,2,1,0:T(2,128)(2,1)} %copy.195), calls=%async_computation.1 | async-start | bytes 3145728 | tf_op jit(solution)/shard_map/all_to_all | solution.py:146
  274.6 39.1 %all-gather.1 = bf16[32,12,192]{2,1,0:T(8,128)(2,1)S(1)} all-gather(bf16[1,12,192]{2,1,0:T(8,128)(2,1)S(1)} %bitcast.145), channel_id=1, replica_groups=mesh['fsdp'=32,'feat'=4] {'fsdp'}, dimensions={0}, use_global_device_ids=true | all-gather | bytes 152064 | tf_op jit(solution)/shard_map/all_gather | solution.py:125
  313.8 22.8 %all-gather = bf16[32,6,384]{2,1,0:T(8,128)(2,1)S(1)} all-gather(bf16[1,6,384]{2,1,0:T(8,128)(2,1)S(1)} %bitcast.146), channel_id=1, replica_groups=mesh['fsdp'=32,'feat'=4] {'fsdp'}, dimensions={0}, use_global_device_ids=true | all-gather | bytes 152064 | tf_op jit(solution)/shard_map/all_gather | solution.py:124
  339.6 5.1 %multiply_reduce_fusion = f32[12,128,2]{2,0,1:T(8,128)} fusion(bf16[128,12,1,2,192]{4,3,1,0,2:T(2,128)(2,1)S(1)} %bitcast.137, f32[12,128,2]{2,0,1:T(8,128)S(1)} %broadcast_multiply_fusion), kind=kLoop, calls=%fused_computation.188 | loop fusion | flops 2356224 | bytes 1204224 | tf_op jit(solution)/shard_map/reduce_sum | solution.py:15
  347.3 3.4 reshape.240
  350.8 3.4 reshape.239
  362.0 5.6 %fusion.235 = f32[3072,192]{0,1:T(8,128)} fusion(bf16[384,192]{1,0:T(8,128)(2,1)S(1)} %reshape.249, bf16[192,384]{1,0:T(8,128)(2,1)S(1)} %reshape.247, f32[3072,192]{1,0:T(8,128)} %reshape.240, f32[192]{0:T(256)S(1)} %bitcast.149, f32[3072]{0:T(1024)S(1)} %rsqrt.30, f32[3072]{0:T(1024)S(1)} %div.133), kind=kOutput, calls=%fused_computation.226 | convolution fusion | flops 918945792 | bytes 5038848 | tf_op jit(solution)/shard_map/dot_general | solution.py:107
  (159 shorter events, 177.1 us)
Async XLA Ops:
  0.0 29.8 %copy-start.18 = (f32[3,192]{1,0:T(4,128)S(1)}, f32[3,192]{1,0:T(4,128)}, u32[]{:S(2)}) copy-start(f32[3,192]{1,0:T(4,128)} %param.13) | copy-start | bytes 6916
  0.0 30.4 %copy-start.2 = (bf16[12,256,192]{1,2,0:T(8,128)(2,1)S(1)}, bf16[12,256,192]{1,2,0:T(8,128)(2,1)}, u32[]{:S(2)}) copy-start(bf16[12,256,192]{1,2,0:T(8,128)(2,1)} %param.9) | copy-start | bytes 3538948
  40.0 3.8 %copy-start.7 = (bf16[1,192,192]{2,0,1:T(2,128)(2,1)S(1)}, bf16[1,192,192]{2,0,1:T(2,128)(2,1)}, u32[]{:S(2)}) copy-start(bf16[1,192,192]{2,0,1:T(2,128)(2,1)} %get-tuple-element.118) | copy-start | bytes 221188
  64.7 2.9 copy-start.15
  67.6 2.4 copy-start.14
  67.6 2.9 copy-start.24
  72.6 2.0 copy-start.22
  82.6 9.4 %copy-start.6 = (bf16[1,192,192]{2,0,1:T(2,128)(2,1)S(1)}, bf16[1,192,192]{2,0,1:T(2,128)(2,1)}, u32[]{:S(2)}) copy-start(bf16[1,192,192]{2,0,1:T(2,128)(2,1)} %get-tuple-element.113) | copy-start | bytes 221188
  84.9 32.1 %all-to-all-start = ((bf16[12,128,2,192]{3,2,0,1:T(2,128)(2,1)}), bf16[12,128,2,192]{3,2,0,1:T(2,128)(2,1)S(1)}, u32[]{:S(2)}, u32[]{:S(2)}) async-start(bf16[12,128,2,192]{3,2,0,1:T(2,128)(2,1)} %copy.182), calls=%async_computation | async-start | bytes 3145728 | tf_op jit(solution)/shard_map/all_to_all | solution.py:138
  117.0 6.0 %copy-start = (bf16[12,128,2,192]{3,2,0,1:T(2,128)(2,1)}, bf16[12,128,2,192]{3,2,0,1:T(2,128)(2,1)S(1)}, u32[]{:S(2)}) copy-start(bf16[12,128,2,192]{3,2,0,1:T(2,128)(2,1)S(1)} %all-to-all-done) | copy-start | bytes 3538948
  123.1 5.4 %copy-start.10 = (bf16[1,192,192]{2,0,1:T(2,128)(2,1)S(1)}, bf16[1,192,192]{2,0,1:T(2,128)(2,1)}, u32[]{:S(2)}) copy-start(bf16[1,192,192]{2,0,1:T(2,128)(2,1)} %get-tuple-element.120) | copy-start | bytes 221188
  131.9 7.1 %copy-start.9 = (bf16[1,192,192]{2,0,1:T(2,128)(2,1)S(1)}, bf16[1,192,192]{2,0,1:T(2,128)(2,1)}, u32[]{:S(2)}) copy-start(bf16[1,192,192]{2,0,1:T(2,128)(2,1)} %get-tuple-element.119) | copy-start | bytes 221188
  142.3 7.0 %copy-start.8 = (bf16[1,192,192]{2,0,1:T(2,128)(2,1)S(1)}, bf16[1,192,192]{2,0,1:T(2,128)(2,1)}, u32[]{:S(2)}) copy-start(bf16[1,192,192]{2,0,1:T(2,128)(2,1)} %get-tuple-element.114) | copy-start | bytes 221188
  153.5 3.1 copy-start.5
  188.6 3.1 copy-start.5
  223.6 3.1 copy-start.5
  258.4 2.5 copy-start.1
  261.9 3.4 copy-start.11
  267.8 6.8 %copy-start.16 = (bf16[12,192]{1,0:T(8,128)(2,1)S(1)}, bf16[12,192]{1,0:T(8,128)(2,1)}, u32[]{:S(2)}) copy-start(bf16[12,192]{1,0:T(8,128)(2,1)} %param.12) | copy-start | bytes 13828
  267.8 46.0 %copy-start.17 = (bf16[6,384]{1,0:T(8,128)(2,1)S(1)}, bf16[6,384]{1,0:T(8,128)(2,1)}, u32[]{:S(2)}) copy-start(bf16[6,384]{1,0:T(8,128)(2,1)} %param.11) | copy-start | bytes 13828
  270.7 66.0 %all-to-all-start.1 = ((bf16[1536,1,2,192]{3,2,1,0:T(2,128)(2,1)}), bf16[1536,1,2,192]{3,2,1,0:T(2,128)(2,1)S(1)}, u32[]{:S(2)}, u32[]{:S(2)}) async-start(bf16[1536,1,2,192]{3,2,1,0:T(2,128)(2,1)} %copy.195), calls=%async_computation.1 | async-start | bytes 3145728 | tf_op jit(solution)/shard_map/all_to_all | solution.py:146
  354.2 5.6 %copy-start.3 = (f32[12,256,192]{2,1,0:T(8,128)S(1)}, f32[12,256,192]{2,1,0:T(8,128)}, u32[]{:S(2)}) copy-start(f32[12,256,192]{2,1,0:T(8,128)} %reshape.239) | copy-start | bytes 7077892
  358.3 3.7 copy-start.19
  362.0 5.6 %copy-start.4 = (f32[12,256,192]{1,2,0:T(8,128)S(1)}, f32[12,256,192]{1,2,0:T(8,128)}, u32[]{:S(2)}) copy-start(f32[12,256,192]{1,2,0:T(8,128)} %copy.203) | copy-start | bytes 7077892
  (5 other events, 7.7 us)
where the time goes:
time: 378 us; the launch traced here: 371 us
  matrix products  143 us (38%)
  blocking collectives  89.6 us (24%)
  local copies, waits for them, and re-layouts  74.2 us (20%)
  other arithmetic  26.4 us (7%)
  waiting for transfers between devices  24.1 us (6%)
  starting transfers between devices  11 us (3%)
    sub x24, matrix products, softmax_rows(): exponent = jnp.exp(masked - row_maximum)  62.1 us
    dot_general x18, matrix products, one_block(): jnp.einsum('tdj,jtn->dtn', attention_probabilities, value_rows[..., train...  59.2 us
    all_gather x1, blocking collectives, local(): lax.all_gather(hidden_down_weight, 'fsdp', axis=0, tiled=True)  39.1 us
    all_gather x1, blocking collectives, local(): lax.all_gather(attn_weights, 'fsdp', axis=1, tiled=True)  27.7 us
    all_to_all x1, waiting for transfers between devices, local(): lax.all_to_all(split_cells, ('fsdp', 'feat'), split_axis=1, concat_axis=0...  24.1 us
    all_gather x1, blocking collectives, local(): lax.all_gather(hidden_up_weight, 'fsdp', axis=0, tiled=True)  22.8 us
    unnamed x55, local copies, waits for them, and re-layouts  18.9 us
    reshape x5, local copies, waits for them, and re-layouts, project(): product.astype(jnp.bfloat16).reshape(normed.shape[:-1] + (weight.shape[1],))  10.6 us
  transfers between devices with their start and end apart: 2, of which 1 were waited for; matrix products, arithmetic and copies ran while one was open for 0% of the time, Pallas kernels for 0%

commit v1 on v0

--- a/solution.py
+++ b/solution.py
@@ -121,7 +121,10 @@
 ):
     weights, w_in, w_out = (
         lax.all_gather(attn_weights, "fsdp", axis=1, tiled=True),
-        lax.all_gather(hidden_up_weight, "fsdp", axis=0, tiled=True),
+        jnp.concatenate(
+            lax.all_to_all(jnp.stack([hidden_up_weight] * lax.axis_size("fsdp")), "fsdp", 0, 0),
+            axis=0,
+        ),
         lax.all_gather(hidden_down_weight, "fsdp", axis=0, tiled=True),
     )
     feat_live = jnp.arange(table_cells.shape[1]) < feature_count[0]

time: 378 us -> 363 us (0.960)
  blocking collectives: 89.6 us -> 66.7 us
  local copies, waits for them, and re-layouts: 74.2 us -> 83 us
  other arithmetic: 26.4 us -> 17.7 us
  starting transfers between devices: 11 us -> 19.4 us
    all_gather x1 -> x0, blocking collectives: 22.8 us -> none  [local(): lax.all_gather(hidden_up_weight, 'fsdp', axis=0, tiled=True)]
    convert_element_type x1 -> x3, local copies, waits for them, and re-layouts: 1.52 us -> 8.49 us  [normalize(): return (centered * lax.rsqrt(variance + EPS) * gain).astype(jnp.bfloat16)]
    reduce_sum x3, other arithmetic: 9.5 us -> 4.67 us  [normalize(): variance = jnp.mean(centered * centered, axis=-1, keepdims=True)]
    all_to_all x0 -> x1, starting transfers between devices: none -> 4.56 us  [local(): lax.all_to_all(jnp.stack([hidden_up_weight] * lax.axis_size('fsdp')), 'fs...]
    all_to_all x1, starting transfers between devices: 3.85 us -> 7.66 us  [local(): lax.all_to_all(at_owners, ('fsdp', 'feat'), split_axis=0, concat_axis=1,...]
    unnamed x55 -> x58, local copies, waits for them, and re-layouts: 18.9 us -> 20.8 us
  transfers between devices with their start and end apart: 2 -> 3, of which waited for: 1 -> 1; matrix products, arithmetic and copies ran while one was open for 0% -> 44% of each run, Pallas kernels for 0% -> 0%
where the time goes in v1:
time: 363 us; the launch traced here: 356 us
  matrix products  143 us (39%)
  local copies, waits for them, and re-layouts  83 us (23%)
  blocking collectives  66.7 us (18%)
  waiting for transfers between devices  24.2 us (7%)
  starting transfers between devices  19.4 us (5%)
  other arithmetic  17.7 us (5%)
    sub x24, matrix products, softmax_rows(): exponent = jnp.exp(masked - row_maximum)  62.1 us
    dot_general x18, matrix products, one_block(): jnp.einsum('tdj,jtn->dtn', attention_probabilities, value_rows[..., train...  59.1 us
    all_gather x1, blocking collectives, local(): lax.all_gather(hidden_down_weight, 'fsdp', axis=0, tiled=True)  39 us
    all_gather x1, blocking collectives, local(): lax.all_gather(attn_weights, 'fsdp', axis=1, tiled=True)  27.7 us
    all_to_all x1, waiting for transfers between devices, local(): lax.all_to_all(split_cells, ('fsdp', 'feat'), split_axis=1, concat_axis=0...  24.2 us
    unnamed x58, local copies, waits for them, and re-layouts  20.8 us
    convert_element_type x4, local copies, waits for them, and re-layouts, feed_forward(): value_rows.astype(jnp.float32)  13.3 us
    reshape x5, local copies, waits for them, and re-layouts, project(): product.astype(jnp.bfloat16).reshape(normed.shape[:-1] + (weight.shape[1],))  10.5 us
  transfers between devices with their start and end apart: 3, of which 1 were waited for; matrix products, arithmetic and copies ran while one was open for 44% of the time, Pallas kernels for 0%

profile of v1, /device:TPU:1, one launch (start us, length us, event | category | flops | bytes accessed | tf_op | source)
XLA Modules:
  0.0 355.7 jit_solution(428778431032061849)
XLA Ops:
  0.0 27.7 %all_gather.6 = bf16[8,192,192]{2,0,1:T(8,128)(2,1)S(1)} all-gather(bf16[8,6,192]{2,0,1:T(8,128)(2,1)} %param.10), channel_id=1, replica_groups=mesh['fsdp'=32,'feat'=4] {'fsdp'}, dimensions={1}, use_global_device_ids=true | all-gather | bytes 608256 | tf_op jit(solution)/shard_map/all_gather | solution.py:123
  47.0 3.9 %fusion.410 = (f32[12,256]{1,0:T(8,128)S(1)}, f32[12,256,256]{1,2,0:T(8,128)}) fusion(pred[256]{0:T(512)(128)(4,1)S(1)} %iota_compare_fusion.1, bf16[12,256,32]{1,0,2:T(8,128)(2,1)} %get-tuple-element.136, bf16[12,256,32]{1,0,2:T(8,128)(2,1)} %get-tuple-element.106), kind=kOutput, calls=%fused_computation.349 | convolution fusion | flops 53477632 | bytes 3551488 | tf_op jit(solution)/shard_map/sub | solution.py:22
  50.9 4.0 %fusion.419 = (f32[12,256]{1,0:T(8,128)S(1)}, f32[12,256,256]{1,2,0:T(8,128)}) fusion(pred[256]{0:T(512)(128)(4,1)S(1)} %iota_compare_fusion.1, bf16[12,256,32]{1,0,2:T(8,128)(2,1)} %get-tuple-element.137, bf16[12,256,32]{1,0,2:T(8,128)(2,1)} %get-tuple-element.105), kind=kOutput, calls=%fused_computation.350 | convolution fusion | flops 53477632 | bytes 3551488 | tf_op jit(solution)/shard_map/sub | solution.py:22
  54.9 4.0 %fusion.428 = (f32[12,256]{1,0:T(8,128)S(1)}, f32[12,256,256]{1,2,0:T(8,128)}) fusion(pred[256]{0:T(512)(128)(4,1)S(1)} %iota_compare_fusion.1, bf16[12,256,32]{1,0,2:T(8,128)(2,1)} %get-tuple-element.138, bf16[12,256,32]{1,0,2:T(8,128)(2,1)} %get-tuple-element.104), kind=kOutput, calls=%fused_computation.351 | convolution fusion | flops 53477632 | bytes 3551488 | tf_op jit(solution)/shard_map/sub | solution.py:22
  84.8 7.2 %all-to-all-start = ((bf16[12,128,2,192]{3,2,0,1:T(2,128)(2,1)}), bf16[12,128,2,192]{3,2,0,1:T(2,128)(2,1)S(1)}, u32[]{:S(2)}, u32[]{:S(2)}) async-start(bf16[12,128,2,192]{3,2,0,1:T(2,128)(2,1)} %copy.177), calls=%async_computation | async-start | bytes 3145728 | tf_op jit(solution)/shard_map/all_to_all | solution.py:141
  92.8 24.2 %all-to-all-done = bf16[12,128,2,192]{3,2,0,1:T(2,128)(2,1)S(1)} async-done(((bf16[12,128,2,192]{3,2,0,1:T(2,128)(2,1)}), bf16[12,128,2,192]{3,2,0,1:T(2,128)(2,1)S(1)}, u32[]{:S(2)}, u32[]{:S(2)}) %all-to-all-start) | async-done | bytes 1179680 | tf_op jit(solution)/shard_map/all_to_all | solution.py:141
  117.7 4.6 %all-to-all-start.2 = ((bf16[32,6,384]{2,1,0:T(8,128)(2,1)}), bf16[32,6,384]{2,1,0:T(8,128)(2,1)}, u32[]{:S(2)}, u32[]{:S(2)}) async-start(bf16[32,6,384]{2,1,0:T(8,128)(2,1)} %stack.2), calls=%async_computation.2 | async-start | bytes 393216 | tf_op jit(solution)/shard_map/all_to_all | solution.py:125
  124.1 4.0 %multiply_reduce_fusion = f32[128,12,2]{2,1,0:T(8,128)S(1)} fusion(bf16[12,128,2,192]{3,2,0,1:T(2,128)(2,1)S(1)} %all-to-all-done, f32[128,12,2]{2,1,0:T(8,128)S(1)} %broadcast_multiply_fusion), kind=kLoop, calls=%fused_computation.187 | loop fusion | flops 2356224 | bytes 1204224 | tf_op jit(solution)/shard_map/reduce_sum | solution.py:15
  128.3 3.9 %multiply_convert_fusion = bf16[128,12,1,2,192]{4,3,1,0,2:T(2,128)(2,1)S(1)} fusion(bf16[12,128,2,192]{3,2,0,1:T(2,128)(2,1)S(1)} %all-to-all-done, f32[192]{0:T(256)S(1)} %bitcast.145, f32[128,12,2]{2,1,0:T(8,128)S(1)} %add_rsqrt_fusion, f32[128,12,2]{2,1,0:T(8,128)S(1)} %broadcast_multiply_fusion), kind=kLoop, calls=%fused_computation.186 | loop fusion | flops 2949120 | bytes 2384640 | tf_op jit(solution)/shard_map/convert_element_type | solution.py:16
  139.3 4.9 %copy.185 = bf16[1536,2,192]{0,2,1:T(8,128)(2,1)} copy(bf16[1536,2,192]{2,1,0:T(2,128)(2,1)} %reshape.246) | data formatting | bytes 2359296
  149.7 4.9 %copy.186 = bf16[1536,2,192]{0,2,1:T(8,128)(2,1)} copy(bf16[1536,2,192]{2,1,0:T(2,128)(2,1)} %reshape.247) | data formatting | bytes 2359296
  157.9 105.5 %while.11 = (s32[]{:T(128)}, bf16[3,512,2,192]{1,3,2,0:T(8,128)(2,1)}, bf16[3,512,2,192]{1,3,2,0:T(8,128)(2,1)S(1)}, bf16[1536,2,192]{0,2,1:T(8,128)(2,1)}, bf16...) while((s32[]{:T(128)}, bf16[3,512,2,192]{1,3,2,0:T(8,128)(2,1)}, ...), condition=%wide.region_29.30_spmd.clone, body=%wide.region_16.29_spmd.clone.sunk | while | flops 1897096704 | bytes 11085937 | solution.py:98
  167.3 3.3 fusion.550
  183.6 3.3 fusion.556
  189.0 3.3 fusion.558
  196.9 3.3 fusion.548
  267.0 3.3 copy.189
  275.7 7.7 %all-to-all-start.1 = ((bf16[1536,1,2,192]{3,2,1,0:T(2,128)(2,1)}), bf16[1536,1,2,192]{3,2,1,0:T(2,128)(2,1)S(1)}, u32[]{:S(2)}, u32[]{:S(2)}) async-start(bf16[1536,1,2,192]{3,2,1,0:T(2,128)(2,1)} %copy.190), calls=%async_computation.1 | async-start | bytes 3145728 | tf_op jit(solution)/shard_map/all_to_all | solution.py:149
  283.4 39.0 %all-gather = bf16[32,12,192]{2,1,0:T(8,128)(2,1)S(1)} all-gather(bf16[1,12,192]{2,1,0:T(8,128)(2,1)S(1)} %bitcast.142), channel_id=1, replica_groups=mesh['fsdp'=32,'feat'=4] {'fsdp'}, dimensions={0}, use_global_device_ids=true | all-gather | bytes 152064 | tf_op jit(solution)/shard_map/all_gather | solution.py:128
  326.0 3.8 %copy.191 = f32[128,12,1,2,192]{0,4,3,2,1:T(8,128)S(1)} copy(bf16[128,12,1,2,192]{4,3,1,0,2:T(2,128)(2,1)} %bitcast.138) | data formatting | bytes 3538944 | tf_op jit(solution)/shard_map/convert_element_type | solution.py:107
  333.8 4.1 %convert_element_type.222 = bf16[3072,192]{1,0:T(8,128)(2,1)} reshape(bf16[12,128,1,2,192]{4,3,1,0,2:T(2,128)(2,1)} %copy.193) | data formatting | bytes 2359296 | tf_op jit(solution)/shard_map/convert_element_type | solution.py:16
  337.9 3.4 copy.192
  341.3 3.9 %reshape.252 = f32[12,256,192]{2,1,0:T(8,128)S(1)} reshape(f32[12,128,1,2,192]{4,3,1,0,2:T(2,128)} %copy.192) | data formatting | bytes 4718592 | tf_op jit(solution)/shard_map/convert_element_type | solution.py:107
  347.4 5.0 %fusion.235 = f32[3072,192]{0,1:T(8,128)} fusion(bf16[384,192]{1,0:T(8,128)(2,1)S(1)} %copy-done.16, bf16[3072,192]{1,0:T(8,128)(2,1)} %convert_element_type.222, bf16[192,384]{1,0:T(8,128)(2,1)S(1)} %copy-done.17), kind=kOutput, calls=%fused_computation.225 | convolution fusion | flops 916586496 | bytes 3833856 | tf_op jit(solution)/shard_map/dot_general | solution.py:107
  (163 shorter events, 177.3 us)
Async XLA Ops:
  0.0 29.8 %copy-start.21 = (f32[3,192]{1,0:T(4,128)S(1)}, f32[3,192]{1,0:T(4,128)}, u32[]{:S(2)}) copy-start(f32[3,192]{1,0:T(4,128)} %param.13) | copy-start | bytes 6916
  0.0 30.4 %copy-start.2 = (bf16[12,256,192]{1,2,0:T(8,128)(2,1)S(1)}, bf16[12,256,192]{1,2,0:T(8,128)(2,1)}, u32[]{:S(2)}) copy-start(bf16[12,256,192]{1,2,0:T(8,128)(2,1)} %param.9) | copy-start | bytes 3538948
  40.0 3.8 %copy-start.7 = (bf16[1,192,192]{2,0,1:T(2,128)(2,1)S(1)}, bf16[1,192,192]{2,0,1:T(2,128)(2,1)}, u32[]{:S(2)}) copy-start(bf16[1,192,192]{2,0,1:T(2,128)(2,1)} %get-tuple-element.118) | copy-start | bytes 221188
  64.7 2.9 copy-start.15
  67.6 2.4 copy-start.14
  67.6 2.9 copy-start.26
  82.6 9.5 %copy-start.6 = (bf16[1,192,192]{2,0,1:T(2,128)(2,1)S(1)}, bf16[1,192,192]{2,0,1:T(2,128)(2,1)}, u32[]{:S(2)}) copy-start(bf16[1,192,192]{2,0,1:T(2,128)(2,1)} %get-tuple-element.113) | copy-start | bytes 221188
  82.6 34.4 %copy-start.19 = (bf16[6,384]{1,0:T(8,128)(2,1)S(1)}, bf16[6,384]{1,0:T(8,128)(2,1)}, u32[]{:S(2)}) copy-start(bf16[6,384]{1,0:T(8,128)(2,1)} %param.11) | copy-start | bytes 13828
  84.8 32.1 %all-to-all-start = ((bf16[12,128,2,192]{3,2,0,1:T(2,128)(2,1)}), bf16[12,128,2,192]{3,2,0,1:T(2,128)(2,1)S(1)}, u32[]{:S(2)}, u32[]{:S(2)}) async-start(bf16[12,128,2,192]{3,2,0,1:T(2,128)(2,1)} %copy.177), calls=%async_computation | async-start | bytes 3145728 | tf_op jit(solution)/shard_map/all_to_all | solution.py:141
  117.0 11.3 %copy-start = (bf16[12,128,2,192]{3,2,0,1:T(2,128)(2,1)}, bf16[12,128,2,192]{3,2,0,1:T(2,128)(2,1)S(1)}, u32[]{:S(2)}) copy-start(bf16[12,128,2,192]{3,2,0,1:T(2,128)(2,1)S(1)} %all-to-all-done) | copy-start | bytes 3538948
  117.7 158.0 %all-to-all-start.2 = ((bf16[32,6,384]{2,1,0:T(8,128)(2,1)}), bf16[32,6,384]{2,1,0:T(8,128)(2,1)}, u32[]{:S(2)}, u32[]{:S(2)}) async-start(bf16[32,6,384]{2,1,0:T(8,128)(2,1)} %stack.2), calls=%async_computation.2 | async-start | bytes 393216 | tf_op jit(solution)/shard_map/all_to_all | solution.py:125
  128.3 5.4 %copy-start.10 = (bf16[1,192,192]{2,0,1:T(2,128)(2,1)S(1)}, bf16[1,192,192]{2,0,1:T(2,128)(2,1)}, u32[]{:S(2)}) copy-start(bf16[1,192,192]{2,0,1:T(2,128)(2,1)} %get-tuple-element.120) | copy-start | bytes 221188
  137.1 7.1 %copy-start.9 = (bf16[1,192,192]{2,0,1:T(2,128)(2,1)S(1)}, bf16[1,192,192]{2,0,1:T(2,128)(2,1)}, u32[]{:S(2)}) copy-start(bf16[1,192,192]{2,0,1:T(2,128)(2,1)} %get-tuple-element.119) | copy-start | bytes 221188
  147.5 7.0 %copy-start.8 = (bf16[1,192,192]{2,0,1:T(2,128)(2,1)S(1)}, bf16[1,192,192]{2,0,1:T(2,128)(2,1)}, u32[]{:S(2)}) copy-start(bf16[1,192,192]{2,0,1:T(2,128)(2,1)} %get-tuple-element.114) | copy-start | bytes 221188
  158.8 3.1 copy-start.5
  193.8 3.1 copy-start.5
  228.9 3.1 copy-start.5
  263.4 2.5 copy-start.1
  267.0 3.4 copy-start.11
  272.8 10.6 %copy-start.18 = (bf16[12,192]{1,0:T(8,128)(2,1)S(1)}, bf16[12,192]{1,0:T(8,128)(2,1)}, u32[]{:S(2)}) copy-start(bf16[12,192]{1,0:T(8,128)(2,1)} %param.12) | copy-start | bytes 13828
  275.7 49.1 %all-to-all-start.1 = ((bf16[1536,1,2,192]{3,2,1,0:T(2,128)(2,1)}), bf16[1536,1,2,192]{3,2,1,0:T(2,128)(2,1)S(1)}, u32[]{:S(2)}, u32[]{:S(2)}) async-start(bf16[1536,1,2,192]{3,2,1,0:T(2,128)(2,1)} %copy.190), calls=%async_computation.1 | async-start | bytes 3145728 | tf_op jit(solution)/shard_map/all_to_all | solution.py:149
  345.2 2.2 copy-start.16
  345.2 2.2 copy-start.17
  347.4 5.0 %copy-start.3 = (f32[12,256,192]{1,2,0:T(8,128)S(1)}, f32[12,256,192]{1,2,0:T(8,128)}, u32[]{:S(2)}) copy-start(f32[12,256,192]{1,2,0:T(8,128)} %copy.194) | copy-start | bytes 7077892
  (8 other events, 11.4 us)
